TPU v7x, 512 devices: a whole 4x8x8 slice. The times are simulated.
512 devices in a mesh: lat: 64 (over z_hi, y, core), wave: 8 (over x, z_lo).
Axes of the slice: x: 4, y: 8, z: 8 (z_hi: 4, z_lo: 2; z = z_hi * 2 + z_lo), core: 2. Of those that a mesh axis runs over, the one named last changes fastest.
Arguments:
- grid_field: float32 [16, 512, 768], P('wave', 'lat'), may hold values from -6 to 6
- row_longitudes: int32 [512], P('lat'), may hold values from 96 to 768, as said below
- owner_order: int32 [384], replicated, may hold values from 0 to 383, each once
- legendre: float32 [512, 384, 384], P('lat'), may hold values from -0.75 to 0.75
- vertical_band: float32 [4, 3, 4], replicated, may hold values from -1.5 to 1.5
Outputs:
- spectral: float32 [384, 384, 2, 16], P('lat', 'wave')
Inputs may be any that keep to these rules, and one draw needn't show every extreme that they name: `row_longitudes`: at least one row has all 768 longitudes. `owner_order`: each zonal wavenumber appears once; wave device g owns the slots g * 384 // 8 onward.
All inputs are finite; a program needn't handle non-finite values.
Results may differ from a plain program's by a relative error of at most 0.0003.
Values sent between devices are 32-bit elements; how exact they have to be, the bound alone decides.
A program may use at most 128 MiB of HBM per device.

v0:
```python
import math
import jax
import jax.numpy as jnp
from jax import lax
from jax.sharding import PartitionSpec as P

MW = 384
NLON = 768
FIELDS = 4
LEVELS = 4
NN = 384


def row_fourier(wavenumbers, row_values, row_points):
    columns = jnp.arange(NLON, dtype=jnp.int32)
    phase_steps = wavenumbers[None, :] * columns[:, None] % row_points
    phases = phase_steps.astype(jnp.float32) * (2.0 * math.pi / row_points.astype(jnp.float32))
    active = (columns[:, None] < row_points) & (2 * wavenumbers[None, :] < row_points)
    norm_factor = 1.0 / jnp.sqrt(row_points.astype(jnp.float32))
    cosine = jnp.where(active, jnp.cos(phases), 0.0) * norm_factor
    sine_part = jnp.where(active, -jnp.sin(phases), 0.0) * norm_factor
    transform = jnp.concatenate([cosine, sine_part], axis=1)
    return jnp.dot(
        row_values, transform, precision=lax.Precision.HIGHEST, preferred_element_type=jnp.float32
    )


def vertical(sums, vertical_band, degrees):
    components = sums.reshape(sums.shape[:3] + (FIELDS, LEVELS))
    sub_diagonal = vertical_band[:, 0, :]
    main_diagonal = vertical_band[:, 1, :]
    super_diagonal = vertical_band[:, 2, :]
    zero_level = jnp.zeros_like(components[..., :1])
    level_below = jnp.concatenate([zero_level, components[..., :-1]], axis=-1)
    level_above = jnp.concatenate([components[..., 1:], zero_level], axis=-1)
    coupled = sub_diagonal * level_below + main_diagonal * components + super_diagonal * level_above
    laplace_ratio = (degrees * (degrees + 1.0) / (MW * MW)).reshape(-1, 1, 1, 1, 1)
    return (components + laplace_ratio * coupled).reshape(sums.shape)


def shards(grid_field, row_longitudes, owner_order, legendre, vertical_band):
    local_layers, row_dev, longitudes = grid_field.shape
    wave_devices = lax.axis_size("wave")
    lat_devices = lax.axis_size("lat")
    group_waves = MW // wave_devices
    owned_degrees = NN // lat_devices

    def one_row(pair):
        return row_fourier(owner_order, pair[0], pair[1])

    fourier = lax.map(one_row, (jnp.moveaxis(grid_field, 1, 0), row_longitudes))
    fourier = fourier.reshape(row_dev, local_layers, 2, MW)
    owned = lax.all_to_all(fourier, "wave", split_axis=3, concat_axis=1, tiled=True)
    wave_index = lax.axis_index("wave")
    my_waves = lax.dynamic_slice_in_dim(owner_order, wave_index * group_waves, group_waves, 0)
    degree_ids = jnp.arange(NN, dtype=jnp.int32)
    triangle = degree_ids[None, :] >= my_waves[:, None]
    chosen = jnp.where(triangle[None], jnp.take(legendre, my_waves, axis=1), 0.0)
    sums = lax.psum_scatter(
        jnp.einsum("rkn,rlck->nkcl", chosen, owned, precision=lax.Precision.HIGHEST),
        "lat",
        scatter_dimension=0,
        tiled=True,
    )
    lat_index = lax.axis_index("lat")
    degrees = (lat_index * owned_degrees + jnp.arange(owned_degrees, dtype=jnp.int32)).astype(
        jnp.float32
    )
    return vertical(sums, vertical_band, degrees)


def solution(mesh):
    placed = (P("wave", "lat", None), P("lat"), P(), P("lat", None, None), P())
    return jax.shard_map(
        shards, mesh=mesh, in_specs=placed, out_specs=P("lat", "wave", None, None), check_vma=False
    )
```

profile of v0, /device:TPU:2, one launch (start us, length us, event | category | flops | bytes accessed | tf_op | source)
XLA Modules:
  0.0 390.2 jit_solution(15367746661120501559)
XLA Ops:
  7.4 181.0 %while.10 = (s32[]{:T(128)}, f32[8,2,768]{2,1,0:T(2,128)S(1)}, f32[8,2,768]{2,1,0:T(2,128)S(1)}, s32[8]{0:T(128)}, s32[384]{0:T(512)}, /*index=5*/s32[]{:T(128)}, f32[]{:T(128)}, s32[]{:T(128)}) while((s32[]{:T(128)}, f32[8,2,768]{2,1,0:T(2,128)S(1)}, f32[8,2,768]{2,1,0:T(2,128)S(1)}, s32[8]{0:T(128)}, s32[384]{0:T(512)}, ...), condition=%wide.region_1.2_spmd, body=%wide.region_0.1_spmd.sunk | while | flops 19465736 | bytes 4737457 | solution.py:51
  9.7 1.2 multiply_compare_fusion.2
  12.2 16.6 %fusion.32 = (f32[768,384]{1,0:T(8,128)S(1)}, f32[768,384]{1,0:T(8,128)S(1)}) fusion(f32[]{:T(128)S(6)} %sqrt.4, f32[]{:T(128)S(6)} %div.10, s32[]{:T(128)S(6)} %select_n.63, s32[384]{0:T(512)} %get-tuple-element.107, pred[]{:T(512)S(6)} %lt.79, pred[384]{0:T(512)(128)(4,1)S(1)} %multiply_compare_fusion.2, pred[768]{0:T(1024)(128)(4,1)S(1)} %iota_compare_fusion.3), kind=kLoop, calls=%fused_computation.8.clone.1 | loop fusion | flops 4718592 | bytes 2361997 | tf_op jit(solution)/shard_map/while/body/eval_jaxpr/mul | solution.py:20
  32.4 1.2 multiply_compare_fusion.2
  34.8 16.6 %fusion.32 = (f32[768,384]{1,0:T(8,128)S(1)}, f32[768,384]{1,0:T(8,128)S(1)}) fusion(f32[]{:T(128)S(6)} %sqrt.4, f32[]{:T(128)S(6)} %div.10, s32[]{:T(128)S(6)} %select_n.63, s32[384]{0:T(512)} %get-tuple-element.107, pred[]{:T(512)S(6)} %lt.79, pred[384]{0:T(512)(128)(4,1)S(1)} %multiply_compare_fusion.2, pred[768]{0:T(1024)(128)(4,1)S(1)} %iota_compare_fusion.3), kind=kLoop, calls=%fused_computation.8.clone.1 | loop fusion | flops 4718592 | bytes 2361997 | tf_op jit(solution)/shard_map/while/body/eval_jaxpr/mul | solution.py:20
  55.0 1.2 multiply_compare_fusion.2
  57.4 16.6 %fusion.32 = (f32[768,384]{1,0:T(8,128)S(1)}, f32[768,384]{1,0:T(8,128)S(1)}) fusion(f32[]{:T(128)S(6)} %sqrt.4, f32[]{:T(128)S(6)} %div.10, s32[]{:T(128)S(6)} %select_n.63, s32[384]{0:T(512)} %get-tuple-element.107, pred[]{:T(512)S(6)} %lt.79, pred[384]{0:T(512)(128)(4,1)S(1)} %multiply_compare_fusion.2, pred[768]{0:T(1024)(128)(4,1)S(1)} %iota_compare_fusion.3), kind=kLoop, calls=%fused_computation.8.clone.1 | loop fusion | flops 4718592 | bytes 2361997 | tf_op jit(solution)/shard_map/while/body/eval_jaxpr/mul | solution.py:20
  77.6 1.2 multiply_compare_fusion.2
  80.0 16.6 %fusion.32 = (f32[768,384]{1,0:T(8,128)S(1)}, f32[768,384]{1,0:T(8,128)S(1)}) fusion(f32[]{:T(128)S(6)} %sqrt.4, f32[]{:T(128)S(6)} %div.10, s32[]{:T(128)S(6)} %select_n.63, s32[384]{0:T(512)} %get-tuple-element.107, pred[]{:T(512)S(6)} %lt.79, pred[384]{0:T(512)(128)(4,1)S(1)} %multiply_compare_fusion.2, pred[768]{0:T(1024)(128)(4,1)S(1)} %iota_compare_fusion.3), kind=kLoop, calls=%fused_computation.8.clone.1 | loop fusion | flops 4718592 | bytes 2361997 | tf_op jit(solution)/shard_map/while/body/eval_jaxpr/mul | solution.py:20
  100.2 1.2 multiply_compare_fusion.2
  102.7 16.6 %fusion.32 = (f32[768,384]{1,0:T(8,128)S(1)}, f32[768,384]{1,0:T(8,128)S(1)}) fusion(f32[]{:T(128)S(6)} %sqrt.4, f32[]{:T(128)S(6)} %div.10, s32[]{:T(128)S(6)} %select_n.63, s32[384]{0:T(512)} %get-tuple-element.107, pred[]{:T(512)S(6)} %lt.79, pred[384]{0:T(512)(128)(4,1)S(1)} %multiply_compare_fusion.2, pred[768]{0:T(1024)(128)(4,1)S(1)} %iota_compare_fusion.3), kind=kLoop, calls=%fused_computation.8.clone.1 | loop fusion | flops 4718592 | bytes 2361997 | tf_op jit(solution)/shard_map/while/body/eval_jaxpr/mul | solution.py:20
  122.8 1.2 multiply_compare_fusion.2
  125.3 16.6 %fusion.32 = (f32[768,384]{1,0:T(8,128)S(1)}, f32[768,384]{1,0:T(8,128)S(1)}) fusion(f32[]{:T(128)S(6)} %sqrt.4, f32[]{:T(128)S(6)} %div.10, s32[]{:T(128)S(6)} %select_n.63, s32[384]{0:T(512)} %get-tuple-element.107, pred[]{:T(512)S(6)} %lt.79, pred[384]{0:T(512)(128)(4,1)S(1)} %multiply_compare_fusion.2, pred[768]{0:T(1024)(128)(4,1)S(1)} %iota_compare_fusion.3), kind=kLoop, calls=%fused_computation.8.clone.1 | loop fusion | flops 4718592 | bytes 2361997 | tf_op jit(solution)/shard_map/while/body/eval_jaxpr/mul | solution.py:20
  145.4 1.2 multiply_compare_fusion.2
  147.9 16.6 %fusion.32 = (f32[768,384]{1,0:T(8,128)S(1)}, f32[768,384]{1,0:T(8,128)S(1)}) fusion(f32[]{:T(128)S(6)} %sqrt.4, f32[]{:T(128)S(6)} %div.10, s32[]{:T(128)S(6)} %select_n.63, s32[384]{0:T(512)} %get-tuple-element.107, pred[]{:T(512)S(6)} %lt.79, pred[384]{0:T(512)(128)(4,1)S(1)} %multiply_compare_fusion.2, pred[768]{0:T(1024)(128)(4,1)S(1)} %iota_compare_fusion.3), kind=kLoop, calls=%fused_computation.8.clone.1 | loop fusion | flops 4718592 | bytes 2361997 | tf_op jit(solution)/shard_map/while/body/eval_jaxpr/mul | solution.py:20
  168.0 1.2 multiply_compare_fusion.2
  170.5 16.6 %fusion.32 = (f32[768,384]{1,0:T(8,128)S(1)}, f32[768,384]{1,0:T(8,128)S(1)}) fusion(f32[]{:T(128)S(6)} %sqrt.4, f32[]{:T(128)S(6)} %div.10, s32[]{:T(128)S(6)} %select_n.63, s32[384]{0:T(512)} %get-tuple-element.107, pred[]{:T(512)S(6)} %lt.79, pred[384]{0:T(512)(128)(4,1)S(1)} %multiply_compare_fusion.2, pred[768]{0:T(1024)(128)(4,1)S(1)} %iota_compare_fusion.3), kind=kLoop, calls=%fused_computation.8.clone.1 | loop fusion | flops 4718592 | bytes 2361997 | tf_op jit(solution)/shard_map/while/body/eval_jaxpr/mul | solution.py:20
  189.0 1.8 reshape.70
  190.9 9.2 %all-to-all-start = ((f32[8,1,1536]{2,1,0:T(1,128)}), f32[8,1,1536]{2,1,0:T(1,128)S(1)}, u32[]{:S(2)}, u32[]{:S(2)}) async-start(f32[8,1,1536]{2,1,0:T(1,128)} %reshape.70), calls=%async_computation | async-start | bytes 98304 | tf_op jit(solution)/shard_map/all_to_all | solution.py:53
  200.9 3.2 gather_fusion
  208.0 2.2 convolution_bitcast_fusion
  210.2 6.0 %copy.28 = f32[384,48,2,16]{1,3,2,0:T(8,128)} copy(f32[384,48,2,16]{0,3,2,1:T(8,128)S(1)} %convolution_bitcast_fusion) | data formatting | bytes 4718592 | tf_op jit(solution)/shard_map/rkn,rlck->nkcl/transpose | solution.py:60
  217.0 163.7 %reduce-scatter.2.cloned.1.call-done = f32[6,48,2,16]{1,3,2,0:T(8,128)} async-done(((f32[384,48,2,16]{1,3,2,0:T(8,128)}), f32[6,48,2,16]{1,3,2,0:T(8,128)}) %reduce-scatter.2.cloned.1.call-update) | async-done | bytes 36880 | tf_op jit(solution)/shard_map/reduce_scatter | solution.py:59
  381.7 1.7 multiply_add_fusion
  (46 shorter events, 32.1 us)
Async XLA Ops:
  190.9 14.0 %all-to-all-start = ((f32[8,1,1536]{2,1,0:T(1,128)}), f32[8,1,1536]{2,1,0:T(1,128)S(1)}, u32[]{:S(2)}, u32[]{:S(2)}) async-start(f32[8,1,1536]{2,1,0:T(1,128)} %reshape.70), calls=%async_computation | async-start | bytes 98304 | tf_op jit(solution)/shard_map/all_to_all | solution.py:53
  200.0 180.7 %reduce-scatter.2.cloned.1.call-start = ((), (), s32[]{:S(2)}) async-start(), calls=%async_computation.2 | async-start | bytes 6389760 | tf_op jit(solution)/shard_map/reduce_scatter | solution.py:59
  216.3 0.7 copy-start
Sparse Core Ops, SparseCore 0:
  216.4 164.2 reduce-scatter.1
where the time goes:
time: 391 us; the launch traced here: 390 us
  waiting for transfers between devices  164 us (42%)
  other arithmetic  150 us (38%)
  local copies, waits for them, and re-layouts  26.3 us (7%)
  loops' own time  14.4 us (4%)
  between operations  13.5 us (3%)
  matrix products  12 us (3%)
  starting transfers between devices  9.17 us (2%)
    reduce_scatter x1, waiting for transfers between devices, shards(): lax.psum_scatter(jnp.einsum('rkn,rlck->nkcl', chosen, owned, precision=la...  164 us
    mul x8, other arithmetic, row_fourier(): cosine = jnp.where(active, jnp.cos(phases), 0.0) * norm_factor  133 us
    another operation x1, loops' own time, shards(): fourier = lax.map(one_row, (jnp.moveaxis(grid_field, 1, 0), row_longitudes))  14.4 us
    lt x8, other arithmetic, row_fourier(): 2 * wavenumbers[None, :] < row_points  9.97 us
    dynamic_slice x8, local copies, waits for them, and re-layouts, shards(): fourier = lax.map(one_row, (jnp.moveaxis(grid_field, 1, 0), row_longitudes))  9.87 us
    dot_general x8, matrix products, row_fourier(): jnp.dot(row_values, transform, precision=lax.Precision.HIGHEST, preferred...  9.77 us
    all_to_all x1, starting transfers between devices, shards(): lax.all_to_all(fourier, 'wave', split_axis=3, concat_axis=1, tiled=True)  9.16 us
  transfers between devices with their start and end apart: 2, of which 2 were waited for; matrix products, arithmetic and copies ran while one was open for 1% of the time, Pallas kernels for 0%

commit v1 on v0

--- a/solution.py
+++ b/solution.py
@@ -50,7 +50,10 @@
 
     fourier = lax.map(one_row, (jnp.moveaxis(grid_field, 1, 0), row_longitudes))
     fourier = fourier.reshape(row_dev, local_layers, 2, MW)
-    owned = lax.all_to_all(fourier, "wave", split_axis=3, concat_axis=1, tiled=True)
+    owned = jnp.concatenate(
+        lax.all_to_all(jnp.stack(jnp.split(fourier, lax.axis_size("wave"), axis=3)), "wave", 0, 0),
+        axis=1,
+    )
     wave_index = lax.axis_index("wave")
     my_waves = lax.dynamic_slice_in_dim(owner_order, wave_index * group_waves, group_waves, 0)
     degree_ids = jnp.arange(NN, dtype=jnp.int32)

time: 391 us -> 395 us (1.010)
  no operation moved by 1% of the time
where the time goes in v1:
time: 395 us; the launch traced here: 394 us
  waiting for transfers between devices  164 us (42%)
  other arithmetic  152 us (38%)
  local copies, waits for them, and re-layouts  24.4 us (6%)
  loops' own time  17.5 us (4%)
  between operations  13.5 us (3%)
  matrix products  12 us (3%)
  starting transfers between devices  9.17 us (2%)
    reduce_scatter x1, waiting for transfers between devices, shards(): lax.psum_scatter(jnp.einsum('rkn,rlck->nkcl', chosen, owned, precision=la...  164 us
    mul x8, other arithmetic, row_fourier(): cosine = jnp.where(active, jnp.cos(phases), 0.0) * norm_factor  133 us
    another operation x1, loops' own time, shards(): fourier = lax.map(one_row, (jnp.moveaxis(grid_field, 1, 0), row_longitudes))  17.5 us
    lt x8, other arithmetic, row_fourier(): 2 * wavenumbers[None, :] < row_points  11 us
    dynamic_slice x8, local copies, waits for them, and re-layouts, shards(): fourier = lax.map(one_row, (jnp.moveaxis(grid_field, 1, 0), row_longitudes))  10.6 us
    dot_general x8, matrix products, row_fourier(): jnp.dot(row_values, transform, precision=lax.Precision.HIGHEST, preferred...  9.77 us
    all_to_all x1, starting transfers between devices, shards(): lax.all_to_all(jnp.stack(jnp.split(fourier, lax.axis_size('wave'), axis=3...  9.16 us
  transfers between devices with their start and end apart: 2, of which 2 were waited for; matrix products, arithmetic and copies ran while one was open for 1% of the time, Pallas kernels for 0%

profile of v1, /device:TPU:2, one launch (start us, length us, event | category | flops | bytes accessed | tf_op | source)
XLA Modules:
  0.0 393.5 jit_solution(14180057338981863813)
XLA Ops:
  7.4 186.9 %while.10 = (s32[]{:T(128)}, f32[8,2,768]{2,1,0:T(2,128)S(1)}, f32[8,2,768]{2,1,0:T(2,128)S(1)}, s32[8]{0:T(128)}, s32[384]{0:T(512)}, /*index=5*/s32[]{:T(128)}, f32[]{:T(128)}, s32[]{:T(128)}) while((s32[]{:T(128)}, f32[8,2,768]{2,1,0:T(2,128)S(1)}, f32[8,2,768]{2,1,0:T(2,128)S(1)}, s32[8]{0:T(128)}, s32[384]{0:T(512)}, ...), condition=%wide.region_1.2_spmd, body=%wide.region_0.1_spmd.sunk | while | flops 19465736 | bytes 4737457 | solution.py:51
  7.4 1.3 dynamic_slice.20
  10.1 1.4 multiply_compare_fusion.2
  12.9 16.6 %fusion.33 = (f32[768,384]{1,0:T(8,128)S(1)}, f32[768,384]{1,0:T(8,128)S(1)}) fusion(f32[]{:T(128)S(6)} %sqrt.4, f32[]{:T(128)S(6)} %div.10, s32[]{:T(128)S(6)} %select_n.63, s32[384]{0:T(512)} %get-tuple-element.115, pred[]{:T(512)S(6)} %lt.79, pred[384]{0:T(512)(128)(4,1)S(1)} %multiply_compare_fusion.2, pred[768]{0:T(1024)(128)(4,1)S(1)} %iota_compare_fusion.3), kind=kLoop, calls=%fused_computation.8.clone.1 | loop fusion | flops 4718592 | bytes 2361997 | tf_op jit(solution)/shard_map/while/body/eval_jaxpr/mul | solution.py:20
  33.4 1.4 multiply_compare_fusion.2
  36.3 16.6 %fusion.33 = (f32[768,384]{1,0:T(8,128)S(1)}, f32[768,384]{1,0:T(8,128)S(1)}) fusion(f32[]{:T(128)S(6)} %sqrt.4, f32[]{:T(128)S(6)} %div.10, s32[]{:T(128)S(6)} %select_n.63, s32[384]{0:T(512)} %get-tuple-element.115, pred[]{:T(512)S(6)} %lt.79, pred[384]{0:T(512)(128)(4,1)S(1)} %multiply_compare_fusion.2, pred[768]{0:T(1024)(128)(4,1)S(1)} %iota_compare_fusion.3), kind=kLoop, calls=%fused_computation.8.clone.1 | loop fusion | flops 4718592 | bytes 2361997 | tf_op jit(solution)/shard_map/while/body/eval_jaxpr/mul | solution.py:20
  56.8 1.4 multiply_compare_fusion.2
  59.6 16.6 %fusion.33 = (f32[768,384]{1,0:T(8,128)S(1)}, f32[768,384]{1,0:T(8,128)S(1)}) fusion(f32[]{:T(128)S(6)} %sqrt.4, f32[]{:T(128)S(6)} %div.10, s32[]{:T(128)S(6)} %select_n.63, s32[384]{0:T(512)} %get-tuple-element.115, pred[]{:T(512)S(6)} %lt.79, pred[384]{0:T(512)(128)(4,1)S(1)} %multiply_compare_fusion.2, pred[768]{0:T(1024)(128)(4,1)S(1)} %iota_compare_fusion.3), kind=kLoop, calls=%fused_computation.8.clone.1 | loop fusion | flops 4718592 | bytes 2361997 | tf_op jit(solution)/shard_map/while/body/eval_jaxpr/mul | solution.py:20
  80.1 1.4 multiply_compare_fusion.2
  83.0 16.6 %fusion.33 = (f32[768,384]{1,0:T(8,128)S(1)}, f32[768,384]{1,0:T(8,128)S(1)}) fusion(f32[]{:T(128)S(6)} %sqrt.4, f32[]{:T(128)S(6)} %div.10, s32[]{:T(128)S(6)} %select_n.63, s32[384]{0:T(512)} %get-tuple-element.115, pred[]{:T(512)S(6)} %lt.79, pred[384]{0:T(512)(128)(4,1)S(1)} %multiply_compare_fusion.2, pred[768]{0:T(1024)(128)(4,1)S(1)} %iota_compare_fusion.3), kind=kLoop, calls=%fused_computation.8.clone.1 | loop fusion | flops 4718592 | bytes 2361997 | tf_op jit(solution)/shard_map/while/body/eval_jaxpr/mul | solution.py:20
  103.5 1.4 multiply_compare_fusion.2
  106.4 16.6 %fusion.33 = (f32[768,384]{1,0:T(8,128)S(1)}, f32[768,384]{1,0:T(8,128)S(1)}) fusion(f32[]{:T(128)S(6)} %sqrt.4, f32[]{:T(128)S(6)} %div.10, s32[]{:T(128)S(6)} %select_n.63, s32[384]{0:T(512)} %get-tuple-element.115, pred[]{:T(512)S(6)} %lt.79, pred[384]{0:T(512)(128)(4,1)S(1)} %multiply_compare_fusion.2, pred[768]{0:T(1024)(128)(4,1)S(1)} %iota_compare_fusion.3), kind=kLoop, calls=%fused_computation.8.clone.1 | loop fusion | flops 4718592 | bytes 2361997 | tf_op jit(solution)/shard_map/while/body/eval_jaxpr/mul | solution.py:20
  126.8 1.4 multiply_compare_fusion.2
  129.7 16.6 %fusion.33 = (f32[768,384]{1,0:T(8,128)S(1)}, f32[768,384]{1,0:T(8,128)S(1)}) fusion(f32[]{:T(128)S(6)} %sqrt.4, f32[]{:T(128)S(6)} %div.10, s32[]{:T(128)S(6)} %select_n.63, s32[384]{0:T(512)} %get-tuple-element.115, pred[]{:T(512)S(6)} %lt.79, pred[384]{0:T(512)(128)(4,1)S(1)} %multiply_compare_fusion.2, pred[768]{0:T(1024)(128)(4,1)S(1)} %iota_compare_fusion.3), kind=kLoop, calls=%fused_computation.8.clone.1 | loop fusion | flops 4718592 | bytes 2361997 | tf_op jit(solution)/shard_map/while/body/eval_jaxpr/mul | solution.py:20
  150.2 1.4 multiply_compare_fusion.2
  153.1 16.6 %fusion.33 = (f32[768,384]{1,0:T(8,128)S(1)}, f32[768,384]{1,0:T(8,128)S(1)}) fusion(f32[]{:T(128)S(6)} %sqrt.4, f32[]{:T(128)S(6)} %div.10, s32[]{:T(128)S(6)} %select_n.63, s32[384]{0:T(512)} %get-tuple-element.115, pred[]{:T(512)S(6)} %lt.79, pred[384]{0:T(512)(128)(4,1)S(1)} %multiply_compare_fusion.2, pred[768]{0:T(1024)(128)(4,1)S(1)} %iota_compare_fusion.3), kind=kLoop, calls=%fused_computation.8.clone.1 | loop fusion | flops 4718592 | bytes 2361997 | tf_op jit(solution)/shard_map/while/body/eval_jaxpr/mul | solution.py:20
  173.6 1.4 multiply_compare_fusion.2
  176.4 16.6 %fusion.33 = (f32[768,384]{1,0:T(8,128)S(1)}, f32[768,384]{1,0:T(8,128)S(1)}) fusion(f32[]{:T(128)S(6)} %sqrt.4, f32[]{:T(128)S(6)} %div.10, s32[]{:T(128)S(6)} %select_n.63, s32[384]{0:T(512)} %get-tuple-element.115, pred[]{:T(512)S(6)} %lt.79, pred[384]{0:T(512)(128)(4,1)S(1)} %multiply_compare_fusion.2, pred[768]{0:T(1024)(128)(4,1)S(1)} %iota_compare_fusion.3), kind=kLoop, calls=%fused_computation.8.clone.1 | loop fusion | flops 4718592 | bytes 2361997 | tf_op jit(solution)/shard_map/while/body/eval_jaxpr/mul | solution.py:20
  195.5 9.2 %all-to-all-start = ((f32[8,1,1536]{2,1,0:T(1,128)}), f32[8,1,1536]{2,1,0:T(1,128)S(1)}, u32[]{:S(2)}, u32[]{:S(2)}) async-start(f32[8,1,1536]{2,1,0:T(1,128)} %reshape.78), calls=%async_computation | async-start | bytes 98304 | tf_op jit(solution)/shard_map/all_to_all | solution.py:54
  205.6 3.2 gather_fusion
  211.4 2.2 convolution_bitcast_fusion
  213.6 6.0 %copy.32 = f32[384,48,2,16]{1,3,2,0:T(8,128)} copy(f32[384,48,2,16]{0,3,2,1:T(8,128)S(1)} %convolution_bitcast_fusion) | data formatting | bytes 4718592 | tf_op jit(solution)/shard_map/rkn,rlck->nkcl/transpose | solution.py:63
  220.3 163.7 %reduce-scatter.2.cloned.1.call-done = f32[6,48,2,16]{1,3,2,0:T(8,128)} async-done(((f32[384,48,2,16]{1,3,2,0:T(8,128)}), f32[6,48,2,16]{1,3,2,0:T(8,128)}) %reduce-scatter.2.cloned.1.call-update) | async-done | bytes 36880 | tf_op jit(solution)/shard_map/reduce_scatter | solution.py:62
  385.0 1.7 multiply_add_fusion
  (53 shorter events, 31.7 us)
Async XLA Ops:
  195.5 14.0 %all-to-all-start = ((f32[8,1,1536]{2,1,0:T(1,128)}), f32[8,1,1536]{2,1,0:T(1,128)S(1)}, u32[]{:S(2)}, u32[]{:S(2)}) async-start(f32[8,1,1536]{2,1,0:T(1,128)} %reshape.78), calls=%async_computation | async-start | bytes 98304 | tf_op jit(solution)/shard_map/all_to_all | solution.py:54
  204.7 179.3 %reduce-scatter.2.cloned.1.call-start = ((), (), s32[]{:S(2)}) async-start(), calls=%async_computation.2 | async-start | bytes 6389760 | tf_op jit(solution)/shard_map/reduce_scatter | solution.py:62
  219.6 0.7 copy-start
Sparse Core Ops, SparseCore 0:
  219.7 164.2 reduce-scatter.1
